TPU v7x, 128 devices: a whole 4x4x4 slice. The times are simulated.
128 devices in a mesh: dom: 16 (over x_hi, y, core), vol: 8 (over z, x_lo).
Axes of the slice: x: 4 (x_hi: 2, x_lo: 2; x = x_hi * 2 + x_lo), y: 4, z: 4, core: 2. Of those that a mesh axis runs over, the one named last changes fastest.
Arguments:
- volume: bfloat16 [4, 256, 16384], P(None, 'vol', 'dom'), may hold values from -6 to 6
- images: bfloat16 [8192, 16384], P(('dom', 'vol'))
- defocus: float32 [8192], P(('dom', 'vol')), may hold values from 0.5 to 3
- inv_noise: float32 [16384], replicated, may hold values from 0.004 to 0.04
- class_idx: int32 [8192, 4], P(('dom', 'vol')), may hold values from 0 to 3
- pose_idx: int32 [8192, 4], P(('dom', 'vol')), may hold values from 0 to 23
- slab_offset: int32 [24, 128], replicated, may hold values from -2048 to 2048, as said below
Outputs:
- weights: float32 [8192, 4], P(('dom', 'vol'))
- data_acc: bfloat16 [4, 256, 16384], P(None, 'vol', 'dom')
- weight_acc: bfloat16 [4, 256, 8192], P(None, 'vol', 'dom')
Inputs may be any that keep to these rules, and one draw needn't show every extreme that they name: slab_offset[p, r] = t_p (r - 64) with integer tilts t_p of -32 to 32, both ends taken by some orientation.
All inputs are finite; a program needn't handle non-finite values.
Results may differ from a plain program's by a relative error of at most 0.012.
Values may be sent and summed in bfloat16 or wider, within the bound.
A program may use at most 128 MiB of HBM per device.

v0:
```python
import functools
import math

import jax
import jax.numpy as jnp
import numpy as np
from jax import lax
from jax.experimental import pallas as pl
from jax.experimental.pallas import tpu as pltpu
from jax.sharding import PartitionSpec as P

MESH = pl.DeviceIdType.MESH
F32 = jnp.float32
BF16 = jnp.bfloat16

CLS = 4
NZ = 256
NY = 128
NXH = 64
NX2 = 128
POSES = 24
K = 4
CANDS = 96
THIRD = 32
RING = 4
PLANE = 16

PLACES = (
    (0, 0), (0, 1), (0, 3), (1, 0), (3, 0),
    (0, 2), (2, 0), (1, 1), (1, 3), (3, 1), (3, 3),
    (1, 2), (3, 2), (2, 1), (2, 3), (2, 2),
)
PLACE_OF = {step: i for i, step in enumerate(PLACES)}
BACK_OF = [PLACE_OF[(-a) % 4, (-b) % 4] for a, b in PLACES]
CLASSES = ((0, 5), (5, 11), (11, 16))
CLASS_OF = [0] * 5 + [1] * 6 + [2] * 5


def around(axis, turn, place):
    first, second = PLACES[place]
    return ((turn, first, second), (first, turn, second), (first, second, turn))[axis]


def sine_coefficients(terms):
    nodes = 0.5 * np.cos((np.arange(200) + 0.5) * math.pi / 400)
    table = np.stack([nodes ** (2 * k + 1) for k in range(terms)], axis=1)
    return np.linalg.lstsq(table, np.sin(2 * math.pi * nodes), rcond=None)[0].tolist()


SINE = sine_coefficients(5)
ROUNDER = 12582912.0


def sine_of_turns(turns):
    rest = turns - ((turns + ROUNDER) - ROUNDER)
    square = rest * rest
    value = SINE[-1] * square + SINE[-2]
    for coefficient in SINE[-3::-1]:
        value = value * square + coefficient
    return value * rest


def nt_dot(left, right):
    return lax.dot_general(left, right, (((1,), (1,)), ((), ())), preferred_element_type=F32)


def dot(left, right):
    return jnp.dot(left, right, preferred_element_type=F32)


def kernel(
    volume, images, defocus, inv_noise, class_idx, pose_idx, slab_offset,
    weights_out, data_out, weight_out,
    focus_in, noise, cls_in, pose_in, slab_in,
    imgs, signal, scaled, quad, focus,
    volrow, back,
    meta_own, meta_sib, meta_all,
    sl,
    part_own, part_sib,
    w_all, ctf_sq,
    parts, incoming, sums, last,
    data_send, w_send, w_recv, w_held, sq_held,
    local_sem, sib_send, sib_recv, vol_send, vol_recv, meta_send, meta_recv,
    ag_send, ag_recv, ring_send, ring_recv, w_send_sem, w_recv_sem, rs_send, rs_recv, fin_send, fin_recv,
    out_send, out_recv,
):
    dom = lax.axis_index("dom")
    vol = lax.axis_index("vol")
    x = (dom // 8) * 2 + vol % 2
    y = (dom // 2) % 4
    z = vol // 2
    c = dom % 2
    row = dom * 8 + vol

    def device(px, py, pz, pc):
        return ((px // 2) * 8 + py * 2 + pc, pz * 2 + px % 2)

    def near(dx, dy, dz):
        return (x + dx) % 4, (y + dy) % 4, (z + dz) % 4

    def send(src, dst, send_sem, recv_sem, target):
        pltpu.make_async_remote_copy(
            src_ref=src, dst_ref=dst, send_sem=send_sem, recv_sem=recv_sem,
            device_id=target, device_id_type=MESH,
        ).start()

    under_way = {}

    def due(ref, sem):
        name = object()
        under_way[name] = (ref, sem)

        def now():
            del under_way[name]
            pltpu.make_async_copy(ref, ref, sem).wait()

        return now

    def load(src, dst, sem):
        pltpu.make_async_copy(src, dst, sem).start()
        return due(dst, sem)

    sibling = device(x, y, z, 1 - c)

    def at(steps):
        return device(*near(*steps), c)

    barrier = pltpu.get_barrier_semaphore()
    pl.semaphore_signal(barrier, inc=1, device_id=sibling, device_id_type=MESH)
    for k in range(1, 8):
        pl.semaphore_signal(barrier, inc=1, device_id=(dom, (vol + k) % 8), device_id_type=MESH)
        pl.semaphore_signal(barrier, inc=1, device_id=((dom + 2 * k) % 16, vol), device_id_type=MESH)

    def own_images(b):
        return images.at[:, pl.ds(pl.multiple_of((2 * b + c) * 1024, 1024), 1024)]

    def other_images(b):
        return images.at[:, pl.ds(pl.multiple_of((2 * b + 1 - c) * 1024, 1024), 1024)]

    mine = pl.ds(pl.multiple_of(c * 64, 64), 64)
    own_lanes = pl.ds(pl.multiple_of(vol * 128, 128), 128)
    small = [
        load(class_idx, cls_in, local_sem.at[3]),
        load(pose_idx, pose_in, local_sem.at[4]),
        load(defocus, focus_in, local_sem.at[5]),
        load(slab_offset, slab_in, local_sem.at[6]),
        load(inv_noise, noise, local_sem.at[7]),
    ]
    own_volume = load(volume.at[:, :, own_lanes], volrow.at[vol], local_sem.at[1])
    for b in range(8):
        pltpu.make_async_copy(own_images(b), imgs.at[b, mine], local_sem.at[0]).start()
    local_images = due(imgs.at[:, 0:64], local_sem.at[0])
    for arrived in small:
        arrived()

    pair = (cls_in[...] * POSES + pose_in[...]).astype(F32)
    meta_own[...] = jnp.concatenate(
        [jnp.concatenate([pair, focus_in[...], jnp.zeros((3, 64), F32)], axis=0), jnp.zeros((8, 64), F32)], axis=1
    )

    lane24 = lax.broadcasted_iota(jnp.int32, (POSES, 128), 1)
    offset = jnp.sum(jnp.where(lane24 == row, slab_in[...].astype(F32), 0.0), axis=1, keepdims=True)
    offset = offset.astype(jnp.int32)
    whole = lax.shift_right_arithmetic(offset, 4)
    lower = lax.bitwise_and(whole, NZ - 1)
    upper = lax.bitwise_and(whole + 1, NZ - 1)
    fraction = lax.bitwise_and(offset, 15).astype(F32) * (1.0 / 16.0)
    slab = lax.broadcasted_iota(jnp.int32, (POSES, NZ), 1)
    interp = jnp.where(slab == lower, 1.0 - fraction, 0.0) + jnp.where(slab == upper, fraction, 0.0)
    padded = jnp.concatenate([interp, interp, jnp.zeros((128 - 2 * POSES, NZ), F32)], axis=0)
    back[...] = jnp.transpose(padded).astype(BF16)

    pl.semaphore_wait(barrier, 15)

    vol_steps = ((2, 1), (1, 1), (3, 1), (2, 0), (1, 0), (3, 0), (0, 1))
    members = [((z + dz) % 4) * 2 + (vol + dx) % 2 for dz, dx in vol_steps]
    for pv in members:
        send(
            volume.at[:, :, pl.ds(pl.multiple_of(pv * 128, 128), 128)], volrow.at[vol],
            vol_send, vol_recv, (dom, pv),
        )
    volume_rows = due(volrow.at[0:7], vol_recv)
    due(volrow.at[0:7], vol_send)
    send(meta_own, meta_sib, sib_send.at[0], sib_recv.at[0], sibling)
    sibling_meta = due(meta_sib, sib_recv.at[0])
    due(meta_own, sib_send.at[0])
    for b in range(8):
        send(other_images(b), imgs.at[b, mine], sib_send.at[1], sib_recv.at[1], sibling)
    sibling_images = due(imgs.at[:, 0:64], sib_recv.at[1])
    due(imgs.at[:, 0:64], sib_send.at[1])

    sibling_meta()
    lane8 = lax.broadcasted_iota(jnp.int32, (8, 128), 1)
    first = jnp.where(c == 0, meta_own[...], meta_sib[...])
    second = jnp.where(c == 0, meta_sib[...], meta_own[...])
    meta = jnp.where(lane8 < 64, first, pltpu.roll(second, 64, 1))
    meta_all[0] = meta
    columns = jnp.transpose(jnp.concatenate([meta, jnp.zeros((120, 128), F32)], axis=0))
    focus[...] = jnp.broadcast_to(columns[:, 4:5], (128, 128))

    lane_row = lax.broadcasted_iota(jnp.int32, (1, 128), 1) % NXH
    kx_sq = (lane_row * lane_row).astype(F32)
    turn = 6.0 / (2.0 * math.pi * (NY // 2) ** 2)

    def prepare(step, carry):
        px, py, pz = near(step // 16, (step // 4) % 4, step % 4)
        b = (px // 2) * 4 + py
        v = pz * 2 + px % 2
        r = (2 * b + c) * 8 + v
        ky = jnp.where(r < NY // 2, r, r - NY)
        squares = (kx_sq + (ky * ky).astype(F32)) * turn
        lanes = pl.ds(pl.multiple_of(v * 128, 128), 128)
        group = step // 8
        spot = pl.ds(pl.multiple_of((step % 8) * 128, 128), 128)
        contrast = -sine_of_turns(focus[...] * squares + 0.1 / (2.0 * math.pi))
        seen = contrast * imgs[b, :, lanes].astype(F32)
        level = noise[pl.ds(r, 1), :]
        signal[group, :, spot] = seen.astype(BF16)
        scaled[group, :, spot] = (seen * level).astype(BF16)
        quad[group, :, spot] = (contrast * contrast * (-0.5 * level)).astype(BF16)
        return carry

    local_images()
    sibling_images()
    lax.fori_loop(0, 24, prepare, 0)

    own_volume()
    volume_rows()
    narrow = interp.astype(BF16)
    rows = [
        dot(narrow, jnp.concatenate([volrow[j, g] for j in range(8)], axis=0)) for g in range(CLS)
    ]
    slices = jnp.concatenate(rows, axis=0).astype(BF16)
    for t in range(3):
        sl[t, 0, 0] = slices[t * THIRD : (t + 1) * THIRD]
    for place in (*range(1, 5), *range(15, 4, -1)):
        for t in range(3):
            send(
                sl.at[t, 0, 0], sl.at[t, 0, BACK_OF[place]],
                ag_send, ag_recv.at[t, CLASS_OF[place]], at(around(t, 0, place)),
            )
    planes = [
        [due(sl.at[t, 0, max(low, 1) : high], ag_recv.at[t, i]) for t in range(3)]
        for i, (low, high) in enumerate(CLASSES)
    ]
    due(sl.at[:, 0, 0:15], ag_send)
    lax.fori_loop(24, 44, prepare, 0)

    for i, (low, high) in enumerate(CLASSES):
        for t in range(3):
            planes[i][t]()
            for d in (2, 1, 3):
                send(
                    sl.at[t, 0, low:high], sl.at[t, 4 - d, low:high],
                    ring_send, ring_recv.at[t], at(around(t, d, 0)),
                )
    rest = [due(sl.at[t, 1:4], ring_recv.at[t]) for t in range(3)]
    due(sl.at[:, 1:4], ring_send)
    lax.fori_loop(44, 64, prepare, 0)

    for arrived in rest:
        arrived()

    scores = jnp.zeros((CANDS, 128), F32)
    for group in range(8):
        pieces = []
        for step in range(8 * group, 8 * group + 8):
            dx, dy, dz = step // 16, (step // 4) % 4, step % 4
            pieces.append(
                jnp.concatenate(
                    [
                        sl[0, dx, PLACE_OF[dy, dz]],
                        sl[1, dy, PLACE_OF[dx, dz]],
                        sl[2, dz, PLACE_OF[dx, dy]],
                    ],
                    axis=0,
                )
            )
        band = jnp.concatenate(pieces, axis=1)
        wide_band = band.astype(F32)
        band_sq = (wide_band * wide_band).astype(BF16)
        scores = scores + nt_dot(band, scaled[group]) + nt_dot(band_sq, quad[group])
    sub96 = lax.broadcasted_iota(jnp.int32, (CANDS, 128), 0).astype(F32)
    picked = [
        jnp.sum(jnp.where(sub96 == meta[k : k + 1], scores, 0.0), axis=0, keepdims=True) for k in range(K)
    ]
    part_own[...] = jnp.concatenate(picked + [jnp.zeros((4, 128), F32)], axis=0)
    send(part_own, part_sib, sib_send.at[2], sib_recv.at[2], sibling)
    due(part_own, sib_send.at[2])
    sibling_part = due(part_sib, sib_recv.at[2])
    for place in range(PLANE - 1, -1, -1):
        for d in (2, 1, 3, 0):
            if (d, place) != (0, 0):
                send(
                    meta_all.at[0], meta_all.at[(4 - d) % 4 * PLANE + BACK_OF[place]],
                    meta_send, meta_recv, at(around(0, d, place)),
                )
    due(meta_all.at[0:63], meta_send)
    every_meta = due(meta_all.at[0:63], meta_recv)
    sibling_part()
    both = (part_own[...] + part_sib[...])[0:K]
    best = jnp.max(both, axis=0, keepdims=True)
    grown = jnp.exp(both - best)
    weights = grown / jnp.sum(grown, axis=0, keepdims=True)
    w_all[0] = weights
    w_held[...] = jnp.where(c == 0, weights, pltpu.roll(weights, 64, 1))[:, 0:64]
    load(w_held, weights_out, local_sem.at[8])

    spread = jnp.zeros((CANDS, 128), F32)
    for k in range(K):
        spread = spread + jnp.where(sub96 == meta[k : k + 1], weights[k : k + 1], 0.0)
    spread = spread.astype(BF16)

    for group in range(8):
        band = dot(spread, signal[group]).astype(BF16)
        for i in range(8):
            step = 8 * group + i
            dx, dy, dz = step // 16, (step // 4) % 4, step % 4
            piece = band[:, i * 128 : (i + 1) * 128]
            parts[0, dx, PLACE_OF[dy, dz]] = piece[0:THIRD]
            parts[1, dy, PLACE_OF[dx, dz]] = piece[THIRD : 2 * THIRD]
            parts[2, dz, PLACE_OF[dx, dy]] = piece[2 * THIRD :]
    for i in (2, 1, 0):
        low, high = CLASSES[i]
        for d in (2, 1, 3):
            for t in range(3):
                send(
                    parts.at[t, d, low:high], incoming.at[t, d - 1, low:high],
                    rs_send, rs_recv.at[t, i], at(around(t, d, 0)),
                )
        if i == 2:
            for place in range(PLANE - 1, -1, -1):
                for d in (2, 1, 3, 0):
                    if (d, place) != (0, 0):
                        send(
                            w_all.at[0], w_all.at[(4 - d) % 4 * PLANE + BACK_OF[place]],
                            w_send_sem, w_recv_sem, at(around(0, d, place)),
                        )
            due(w_all.at[0:63], w_send_sem)
            every_w = due(w_all.at[0:63], w_recv_sem)
    rings = [
        [due(incoming.at[t, :, low:high], rs_recv.at[t, i]) for t in range(3)]
        for i, (low, high) in enumerate(CLASSES)
    ]
    due(incoming, rs_send)

    every_meta()
    own_ky = jnp.where(row < NY // 2, row, row - NY)
    sub64 = lax.broadcasted_iota(jnp.int32, (NXH, 128), 0)
    own_squares = (sub64 * sub64 + own_ky * own_ky).astype(F32) * turn

    def square_row(step, carry):
        px = step // PLANE
        pp = step % PLANE
        wave = sine_of_turns(meta_all[step, 4:5, :] * own_squares + 0.1 / (2.0 * math.pi))
        ctf_sq[px, :, pl.ds(pl.multiple_of(pp * 128, 128), 128)] = (wave * wave).astype(BF16)
        return carry

    lax.fori_loop(0, 64, square_row, 0)


    for i in (2, 1, 0):
        low, high = CLASSES[i]
        for t in range(3):
            rings[i][t]()
            for place in range(high - 1, low - 1, -1):
                total = parts[t, 0, place].astype(F32)
                for d in range(3):
                    total = total + incoming[t, d, place].astype(F32)
                sums[t, place] = total.astype(BF16)
                if place > 0:
                    send(
                        sums.at[t, place], last.at[t, BACK_OF[place] - 1],
                        fin_send, fin_recv.at[t], at(around(t, 0, place)),
                    )
    finals = [due(last.at[t], fin_recv.at[t]) for t in range(3)]
    due(last, fin_send)

    every_w()

    def weigh(px, total):
        blocks = []
        for pp in range(PLANE):
            block = jnp.zeros((CANDS, 128), F32)
            for k in range(K):
                block = block + jnp.where(
                    sub96 == meta_all[px * PLANE + pp, k : k + 1, :], w_all[px * PLANE + pp, k : k + 1, :], 0.0
                )
            blocks.append(block.astype(BF16))
        return total + nt_dot(jnp.concatenate(blocks, axis=1), ctf_sq[px])

    weight_slices = lax.fori_loop(0, RING, weigh, jnp.zeros((CANDS, NXH), F32))

    def backproject(sums, width):
        flat = jnp.concatenate([sums[g * POSES : (g + 1) * POSES] for g in range(CLS)], axis=1)
        high = flat.astype(BF16).astype(F32)
        stacked = jnp.concatenate(
            [high, flat - high, jnp.zeros((128 - 2 * POSES, CLS * width), F32)], axis=0
        )
        return dot(back[...], stacked.astype(BF16)).astype(BF16)

    result = backproject(weight_slices, NXH)
    for j in range(8):
        w_send[j] = result[j * 32 : (j + 1) * 32]
    w_recv[vol] = w_send[vol]
    for pv in members:
        send(w_send.at[pv], w_recv.at[vol], out_send.at[0], out_recv.at[0], (dom, pv))
    due(w_send.at[0:7], out_send.at[0])
    weight_rows = due(w_recv.at[0:7], out_recv.at[0])

    for arrived in finals:
        arrived()
    own = []
    for t in range(3):
        total = sums[t, 0].astype(F32)
        for j in range(PLANE - 1):
            total = total + last[t, j].astype(F32)
        own.append(total)
    own = jnp.concatenate(own, axis=0)
    result = backproject(own, NX2)
    for j in range(8):
        for g in range(CLS):
            data_send[j, g] = result[j * 32 : (j + 1) * 32, g * 128 : (g + 1) * 128]
    for pv in members:
        send(data_send.at[pv], data_out.at[:, :, own_lanes], out_send.at[1], out_recv.at[1], (dom, pv))
    due(data_send.at[0:7], out_send.at[1])
    due(data_send.at[0:7], out_recv.at[1])
    load(data_send.at[vol], data_out.at[:, :, own_lanes], local_sem.at[2])

    weight_rows()
    for pair_of in range(4):
        even = w_recv[2 * pair_of].astype(F32)
        odd = w_recv[2 * pair_of + 1].astype(F32)
        for g in range(CLS):
            lanes = slice(g * NXH, (g + 1) * NXH)
            sq_held[g, :, pair_of * 128 : (pair_of + 1) * 128] = jnp.concatenate(
                [even[:, lanes], odd[:, lanes]], axis=1
            ).astype(BF16)

    load(sq_held, weight_out, local_sem.at[9])

    for ref, sem in under_way.values():
        pltpu.make_async_copy(ref, ref, sem).wait()


def place(weights, data, squares, weights_out, data_out, weight_out, w_held, d_held, s_held, sems):
    chain = ((weights, w_held, weights_out), (data, d_held, data_out), (squares, s_held, weight_out))
    inward = [pltpu.make_async_copy(src, held, sems.at[0, i]) for i, (src, held, _) in enumerate(chain)]
    outward = [pltpu.make_async_copy(held, dst, sems.at[1, i]) for i, (_, held, dst) in enumerate(chain)]
    for copy in inward:
        copy.start()
    for first, second in zip(inward, outward):
        first.wait()
        second.start()
    for copy in outward:
        copy.wait()


def body(volume, images, defocus, inv_noise, class_idx, pose_idx, slab_offset):
    anywhere = pl.BlockSpec(memory_space=pl.ANY)
    dma = pltpu.SemaphoreType.DMA
    V = pltpu.VMEM
    weights, data_acc, weight_acc = pl.pallas_call(
        kernel,
        out_shape=(
            jax.ShapeDtypeStruct((K, 64), F32),
            jax.ShapeDtypeStruct((CLS, 32, 1024), BF16),
            jax.ShapeDtypeStruct((CLS, 32, 512), BF16),
        ),
        in_specs=[anywhere] * 7,
        out_specs=(anywhere,) * 3,
        scratch_shapes=[
            V((1, 64), F32), V((NY, NX2), F32), V((K, 64), jnp.int32), V((K, 64), jnp.int32),
            V((POSES, NY), jnp.int32),
            V((8, 128, 1024), BF16), V((8, 128, 1024), BF16), V((8, 128, 1024), BF16),
            V((8, 128, 1024), BF16), V((128, 128), F32),
            V((8, CLS, 32, 128), BF16), V((NZ, 128), BF16),
            V((8, 128), F32), V((8, 128), F32), V((RING * PLANE, 8, 128), F32),
            V((3, RING, PLANE, THIRD, 128), BF16),
            V((8, 128), F32), V((8, 128), F32),
            V((RING * PLANE, K, 128), F32), V((RING, NXH, PLANE * 128), BF16),
            V((3, RING, PLANE, THIRD, 128), BF16), V((3, RING - 1, PLANE, THIRD, 128), BF16),
            V((3, PLANE, THIRD, 128), BF16), V((3, PLANE - 1, THIRD, 128), BF16),
            V((8, CLS, 32, 128), BF16), V((8, 32, CLS * NXH), BF16), V((8, 32, CLS * NXH), BF16),
            V((K, 64), F32), V((CLS, 32, 512), BF16),
            dma((10,)), dma((3,)), dma((3,)), dma, dma, dma, dma,
            dma, dma((3, 3)), dma, dma((3,)), dma, dma, dma, dma((3, 3)), dma, dma((3,)),
            dma((2,)), dma((2,)),
        ],
        compiler_params=pltpu.CompilerParams(
            collective_id=0, has_side_effects=True, vmem_limit_bytes=60 * 2**20
        ),
    )(
        volume, images, defocus.reshape(1, 64), inv_noise.reshape(NY, NX2),
        class_idx.T, pose_idx.T, slab_offset,
    )
    weights, data_acc, weight_acc = pl.pallas_call(
        place,
        out_shape=tuple(jax.ShapeDtypeStruct(a.shape, a.dtype) for a in (weights, data_acc, weight_acc)),
        in_specs=[anywhere] * 3,
        out_specs=(anywhere,) * 3,
        scratch_shapes=[V(a.shape, a.dtype) for a in (weights, data_acc, weight_acc)] + [dma((2, 3))],
        compiler_params=pltpu.CompilerParams(vmem_limit_bytes=60 * 2**20),
    )(weights, data_acc, weight_acc)
    return weights.T, data_acc, weight_acc


def solution(mesh):
    return jax.shard_map(
        body,
        mesh=mesh,
        in_specs=(
            P(None, "vol", "dom"),
            P(("dom", "vol"), None),
            P(("dom", "vol")),
            P(),
            P(("dom", "vol"), None),
            P(("dom", "vol"), None),
            P(),
        ),
        out_specs=(P(("dom", "vol"), None), P(None, "vol", "dom"), P(None, "vol", "dom")),
        check_vma=False,
    )
```

profile of v0, /device:TPU:1, one launch (start us, length us, event | category | flops | bytes accessed | tf_op | source)
XLA Modules:
  0.0 53.3 jit_solution(15301941738381645381)
XLA Ops:
  0.6 50.9 %shard_map.94 = (f32[4,64]{1,0:T(4,128)}, bf16[4,32,1024]{2,1,0:T(8,128)(2,1)}, bf16[4,32,512]{2,1,0:T(8,128)(2,1)}) custom-call(bf16[4,32,1024]{2,1,0:T(8,128)(2,1)} %volume.1, bf16[64,16384]{1,0:T(8,128)(2,1)} %images.1, f32[1,64]{1,0:T(1,128)} %bitcast.8, f32[128,128]{1,0:T(8,128)} %bitcast.5, s32[4,64]{1,0:T(4,128)} %bitcast.6, s32[4,64]{1,0:T(4,128)} %bitcast.7, ...), custom_call_target="tpu_custom_call" | custom-call | tf_op jit(solution)/shard_map/pallas_call | solution.py:463
  51.5 1.7 %shard_map.95 = (f32[4,64]{1,0:T(4,128)}, bf16[4,32,1024]{2,1,0:T(8,128)(2,1)}, bf16[4,32,512]{2,1,0:T(8,128)(2,1)}) custom-call(f32[4,64]{1,0:T(4,128)} %get-tuple-element.9.weights, bf16[4,32,1024]{2,1,0:T(8,128)(2,1)} %get-tuple-element.10.data, bf16[4,32,512]{2,1,0:T(8,128)(2,1)} %get-tuple-element.11.squares), custom_call_target="tpu_custom_call" | custom-call | tf_op jit(solution)/shard_map/pallas_call | solution.py:497
where the time goes:
time: 53.4 us; the launch traced here: 53.3 us
  Pallas kernels  52.6 us (99%)
  between operations  0.64 us (1%)
    pallas_call x1, Pallas kernels, body(): pl.pallas_call(kernel, out_shape=(jax.ShapeDtypeStruct((K, 64), F32), jax...  50.9 us
    pallas_call x1, Pallas kernels, body(): pl.pallas_call(place, out_shape=tuple((jax.ShapeDtypeStruct(a.shape, a.dt...  1.75 us

commit v1 on v0

--- a/solution.py
+++ b/solution.py
@@ -77,12 +77,12 @@
     meta_own, meta_sib, meta_all,
     sl,
     part_own, part_sib,
-    w_all, ctf_sq,
+    w_all, ctf_sq, sq_part, sq_in,
     parts, incoming, sums, last,
     data_send, w_send, w_recv, w_held, sq_held,
     local_sem, sib_send, sib_recv, vol_send, vol_recv, meta_send, meta_recv,
     ag_send, ag_recv, ring_send, ring_recv, w_send_sem, w_recv_sem, rs_send, rs_recv, fin_send, fin_recv,
-    out_send, out_recv,
+    out_send, out_recv, sq_send, sq_recv,
 ):
     dom = lax.axis_index("dom")
     vol = lax.axis_index("vol")
@@ -139,6 +139,10 @@
 
     mine = pl.ds(pl.multiple_of(c * 64, 64), 64)
     own_lanes = pl.ds(pl.multiple_of(vol * 128, 128), 128)
+    own_volume = load(volume.at[:, :, own_lanes], volrow.at[vol], local_sem.at[1])
+    for b in range(8):
+        pltpu.make_async_copy(own_images(b), imgs.at[b, mine], local_sem.at[0]).start()
+    local_images = due(imgs.at[:, 0:64], local_sem.at[0])
     small = [
         load(class_idx, cls_in, local_sem.at[3]),
         load(pose_idx, pose_in, local_sem.at[4]),
@@ -146,30 +150,6 @@
         load(slab_offset, slab_in, local_sem.at[6]),
         load(inv_noise, noise, local_sem.at[7]),
     ]
-    own_volume = load(volume.at[:, :, own_lanes], volrow.at[vol], local_sem.at[1])
-    for b in range(8):
-        pltpu.make_async_copy(own_images(b), imgs.at[b, mine], local_sem.at[0]).start()
-    local_images = due(imgs.at[:, 0:64], local_sem.at[0])
-    for arrived in small:
-        arrived()
-
-    pair = (cls_in[...] * POSES + pose_in[...]).astype(F32)
-    meta_own[...] = jnp.concatenate(
-        [jnp.concatenate([pair, focus_in[...], jnp.zeros((3, 64), F32)], axis=0), jnp.zeros((8, 64), F32)], axis=1
-    )
-
-    lane24 = lax.broadcasted_iota(jnp.int32, (POSES, 128), 1)
-    offset = jnp.sum(jnp.where(lane24 == row, slab_in[...].astype(F32), 0.0), axis=1, keepdims=True)
-    offset = offset.astype(jnp.int32)
-    whole = lax.shift_right_arithmetic(offset, 4)
-    lower = lax.bitwise_and(whole, NZ - 1)
-    upper = lax.bitwise_and(whole + 1, NZ - 1)
-    fraction = lax.bitwise_and(offset, 15).astype(F32) * (1.0 / 16.0)
-    slab = lax.broadcasted_iota(jnp.int32, (POSES, NZ), 1)
-    interp = jnp.where(slab == lower, 1.0 - fraction, 0.0) + jnp.where(slab == upper, fraction, 0.0)
-    padded = jnp.concatenate([interp, interp, jnp.zeros((128 - 2 * POSES, NZ), F32)], axis=0)
-    back[...] = jnp.transpose(padded).astype(BF16)
-
     pl.semaphore_wait(barrier, 15)
 
     vol_steps = ((2, 1), (1, 1), (3, 1), (2, 0), (1, 0), (3, 0), (0, 1))
@@ -181,11 +161,19 @@
         )
     volume_rows = due(volrow.at[0:7], vol_recv)
     due(volrow.at[0:7], vol_send)
+    for b in range(8):
+        send(other_images(b), imgs.at[b, mine], sib_send.at[1], sib_recv.at[1], sibling)
+    for arrived in small:
+        arrived()
+
+    pair = (cls_in[...] * POSES + pose_in[...]).astype(F32)
+    meta_own[...] = jnp.concatenate(
+        [jnp.concatenate([pair, focus_in[...], jnp.zeros((3, 64), F32)], axis=0), jnp.zeros((8, 64), F32)], axis=1
+    )
+
     send(meta_own, meta_sib, sib_send.at[0], sib_recv.at[0], sibling)
     sibling_meta = due(meta_sib, sib_recv.at[0])
     due(meta_own, sib_send.at[0])
-    for b in range(8):
-        send(other_images(b), imgs.at[b, mine], sib_send.at[1], sib_recv.at[1], sibling)
     sibling_images = due(imgs.at[:, 0:64], sib_recv.at[1])
     due(imgs.at[:, 0:64], sib_send.at[1])
 
@@ -195,6 +183,10 @@
     second = jnp.where(c == 0, meta_sib[...], meta_own[...])
     meta = jnp.where(lane8 < 64, first, pltpu.roll(second, 64, 1))
     meta_all[0] = meta
+    for k in range(1, 8):
+        send(meta_all.at[0], meta_all.at[8 - k], meta_send, meta_recv, ((dom + 2 * k) % 16, vol))
+    due(meta_all.at[0:7], meta_send)
+    dom_meta = due(meta_all.at[0:7], meta_recv)
     columns = jnp.transpose(jnp.concatenate([meta, jnp.zeros((120, 128), F32)], axis=0))
     focus[...] = jnp.broadcast_to(columns[:, 4:5], (128, 128))
 
@@ -222,7 +214,19 @@
 
     local_images()
     sibling_images()
-    lax.fori_loop(0, 24, prepare, 0)
+    lax.fori_loop(0, 8, prepare, 0)
+
+    lane24 = lax.broadcasted_iota(jnp.int32, (POSES, 128), 1)
+    offset = jnp.sum(jnp.where(lane24 == row, slab_in[...].astype(F32), 0.0), axis=1, keepdims=True)
+    offset = offset.astype(jnp.int32)
+    whole = lax.shift_right_arithmetic(offset, 4)
+    lower = lax.bitwise_and(whole, NZ - 1)
+    upper = lax.bitwise_and(whole + 1, NZ - 1)
+    fraction = lax.bitwise_and(offset, 15).astype(F32) * (1.0 / 16.0)
+    slab = lax.broadcasted_iota(jnp.int32, (POSES, NZ), 1)
+    interp = jnp.where(slab == lower, 1.0 - fraction, 0.0) + jnp.where(slab == upper, fraction, 0.0)
+    padded = jnp.concatenate([interp, interp, jnp.zeros((128 - 2 * POSES, NZ), F32)], axis=0)
+    back[...] = jnp.transpose(padded).astype(BF16)
 
     own_volume()
     volume_rows()
@@ -244,7 +248,7 @@
         for i, (low, high) in enumerate(CLASSES)
     ]
     due(sl.at[:, 0, 0:15], ag_send)
-    lax.fori_loop(24, 44, prepare, 0)
+    lax.fori_loop(8, 24, prepare, 0)
 
     for i, (low, high) in enumerate(CLASSES):
         for t in range(3):
@@ -256,7 +260,7 @@
                 )
     rest = [due(sl.at[t, 1:4], ring_recv.at[t]) for t in range(3)]
     due(sl.at[:, 1:4], ring_send)
-    lax.fori_loop(44, 64, prepare, 0)
+    lax.fori_loop(24, 64, prepare, 0)
 
     for arrived in rest:
         arrived()
@@ -288,21 +292,16 @@
     send(part_own, part_sib, sib_send.at[2], sib_recv.at[2], sibling)
     due(part_own, sib_send.at[2])
     sibling_part = due(part_sib, sib_recv.at[2])
-    for place in range(PLANE - 1, -1, -1):
-        for d in (2, 1, 3, 0):
-            if (d, place) != (0, 0):
-                send(
-                    meta_all.at[0], meta_all.at[(4 - d) % 4 * PLANE + BACK_OF[place]],
-                    meta_send, meta_recv, at(around(0, d, place)),
-                )
-    due(meta_all.at[0:63], meta_send)
-    every_meta = due(meta_all.at[0:63], meta_recv)
     sibling_part()
     both = (part_own[...] + part_sib[...])[0:K]
     best = jnp.max(both, axis=0, keepdims=True)
     grown = jnp.exp(both - best)
     weights = grown / jnp.sum(grown, axis=0, keepdims=True)
     w_all[0] = weights
+    for k in range(1, 8):
+        send(w_all.at[0], w_all.at[8 - k], w_send_sem, w_recv_sem, ((dom + 2 * k) % 16, vol))
+    due(w_all.at[0:7], w_send_sem)
+    dom_w = due(w_all.at[0:7], w_recv_sem)
     w_held[...] = jnp.where(c == 0, weights, pltpu.roll(weights, 64, 1))[:, 0:64]
     load(w_held, weights_out, local_sem.at[8])
 
@@ -328,36 +327,43 @@
                     parts.at[t, d, low:high], incoming.at[t, d - 1, low:high],
                     rs_send, rs_recv.at[t, i], at(around(t, d, 0)),
                 )
-        if i == 2:
-            for place in range(PLANE - 1, -1, -1):
-                for d in (2, 1, 3, 0):
-                    if (d, place) != (0, 0):
-                        send(
-                            w_all.at[0], w_all.at[(4 - d) % 4 * PLANE + BACK_OF[place]],
-                            w_send_sem, w_recv_sem, at(around(0, d, place)),
-                        )
-            due(w_all.at[0:63], w_send_sem)
-            every_w = due(w_all.at[0:63], w_recv_sem)
     rings = [
         [due(incoming.at[t, :, low:high], rs_recv.at[t, i]) for t in range(3)]
         for i, (low, high) in enumerate(CLASSES)
     ]
     due(incoming, rs_send)
 
-    every_meta()
-    own_ky = jnp.where(row < NY // 2, row, row - NY)
+    dom_meta()
     sub64 = lax.broadcasted_iota(jnp.int32, (NXH, 128), 0)
-    own_squares = (sub64 * sub64 + own_ky * own_ky).astype(F32) * turn
 
     def square_row(step, carry):
-        px = step // PLANE
-        pp = step % PLANE
-        wave = sine_of_turns(meta_all[step, 4:5, :] * own_squares + 0.1 / (2.0 * math.pi))
-        ctf_sq[px, :, pl.ds(pl.multiple_of(pp * 128, 128), 128)] = (wave * wave).astype(BF16)
+        band_row = step // 8
+        k = step % 8
+        r = dom * 8 + band_row
+        ky = jnp.where(r < NY // 2, r, r - NY)
+        squares = (sub64 * sub64 + ky * ky).astype(F32) * turn
+        wave = sine_of_turns(meta_all[k, 4:5, :] * squares + 0.1 / (2.0 * math.pi))
+        ctf_sq[band_row, :, pl.ds(pl.multiple_of(k * 128, 128), 128)] = (wave * wave).astype(BF16)
         return carry
 
     lax.fori_loop(0, 64, square_row, 0)
 
+    dom_w()
+    blocks = []
+    for k in range(8):
+        block = jnp.zeros((CANDS, 128), F32)
+        for j in range(K):
+            block = block + jnp.where(sub96 == meta_all[k, j : j + 1, :], w_all[k, j : j + 1, :], 0.0)
+        blocks.append(block.astype(BF16))
+    blocks = jnp.concatenate(blocks, axis=1)
+    for band_row in range(8):
+        part = nt_dot(blocks, ctf_sq[band_row])
+        sq_part[band_row] = jnp.concatenate([part[0:48], part[48:96]], axis=1).astype(BF16)
+    sq_in[vol] = sq_part[vol]
+    for pv in members:
+        send(sq_part.at[pv], sq_in.at[vol], sq_send, sq_recv, (dom, pv))
+    due(sq_part.at[0:7], sq_send)
+    vol_parts = due(sq_in.at[0:7], sq_recv)
 
     for i in (2, 1, 0):
         low, high = CLASSES[i]
@@ -376,30 +382,21 @@
     finals = [due(last.at[t], fin_recv.at[t]) for t in range(3)]
     due(last, fin_send)
 
-    every_w()
-
-    def weigh(px, total):
-        blocks = []
-        for pp in range(PLANE):
-            block = jnp.zeros((CANDS, 128), F32)
-            for k in range(K):
-                block = block + jnp.where(
-                    sub96 == meta_all[px * PLANE + pp, k : k + 1, :], w_all[px * PLANE + pp, k : k + 1, :], 0.0
-                )
-            blocks.append(block.astype(BF16))
-        return total + nt_dot(jnp.concatenate(blocks, axis=1), ctf_sq[px])
-
-    weight_slices = lax.fori_loop(0, RING, weigh, jnp.zeros((CANDS, NXH), F32))
-
-    def backproject(sums, width):
-        flat = jnp.concatenate([sums[g * POSES : (g + 1) * POSES] for g in range(CLS)], axis=1)
+    vol_parts()
+    folded = sq_in[0].astype(F32)
+    for j in range(1, 8):
+        folded = folded + sq_in[j].astype(F32)
+    weight_slices = jnp.concatenate([folded[:, 0:NXH], folded[:, NXH:]], axis=0)
+
+    def backproject(classes):
+        flat = jnp.concatenate(classes, axis=1)
         high = flat.astype(BF16).astype(F32)
         stacked = jnp.concatenate(
-            [high, flat - high, jnp.zeros((128 - 2 * POSES, CLS * width), F32)], axis=0
+            [high, flat - high, jnp.zeros((128 - 2 * POSES, flat.shape[1]), F32)], axis=0
         )
         return dot(back[...], stacked.astype(BF16)).astype(BF16)
 
-    result = backproject(weight_slices, NXH)
+    result = backproject([weight_slices[g * POSES : (g + 1) * POSES] for g in range(CLS)])
     for j in range(8):
         w_send[j] = result[j * 32 : (j + 1) * 32]
     w_recv[vol] = w_send[vol]
@@ -408,21 +405,21 @@
     due(w_send.at[0:7], out_send.at[0])
     weight_rows = due(w_recv.at[0:7], out_recv.at[0])
 
-    for arrived in finals:
-        arrived()
     own = []
-    for t in range(3):
-        total = sums[t, 0].astype(F32)
-        for j in range(PLANE - 1):
-            total = total + last[t, j].astype(F32)
-        own.append(total)
-    own = jnp.concatenate(own, axis=0)
-    result = backproject(own, NX2)
-    for j in range(8):
-        for g in range(CLS):
-            data_send[j, g] = result[j * 32 : (j + 1) * 32, g * 128 : (g + 1) * 128]
-    for pv in members:
-        send(data_send.at[pv], data_out.at[:, :, own_lanes], out_send.at[1], out_recv.at[1], (dom, pv))
+    for g in range(CLS):
+        while len(own) * THIRD < (g + 1) * POSES:
+            t = len(own)
+            finals[t]()
+            total = sums[t, 0].astype(F32)
+            for j in range(PLANE - 1):
+                total = total + last[t, j].astype(F32)
+            own.append(total)
+        joined = jnp.concatenate(own, axis=0)
+        result = backproject([joined[g * POSES : (g + 1) * POSES]])
+        for j in range(8):
+            data_send[j, g] = result[j * 32 : (j + 1) * 32]
+        for pv in members:
+            send(data_send.at[pv, g], data_out.at[g, :, own_lanes], out_send.at[1], out_recv.at[1], (dom, pv))
     due(data_send.at[0:7], out_send.at[1])
     due(data_send.at[0:7], out_recv.at[1])
     load(data_send.at[vol], data_out.at[:, :, own_lanes], local_sem.at[2])
@@ -475,17 +472,18 @@
             V((8, 128, 1024), BF16), V((8, 128, 1024), BF16), V((8, 128, 1024), BF16),
             V((8, 128, 1024), BF16), V((128, 128), F32),
             V((8, CLS, 32, 128), BF16), V((NZ, 128), BF16),
-            V((8, 128), F32), V((8, 128), F32), V((RING * PLANE, 8, 128), F32),
+            V((8, 128), F32), V((8, 128), F32), V((8, 8, 128), F32),
             V((3, RING, PLANE, THIRD, 128), BF16),
             V((8, 128), F32), V((8, 128), F32),
-            V((RING * PLANE, K, 128), F32), V((RING, NXH, PLANE * 128), BF16),
+            V((8, K, 128), F32), V((8, NXH, 1024), BF16),
+            V((8, 48, 128), BF16), V((8, 48, 128), BF16),
             V((3, RING, PLANE, THIRD, 128), BF16), V((3, RING - 1, PLANE, THIRD, 128), BF16),
             V((3, PLANE, THIRD, 128), BF16), V((3, PLANE - 1, THIRD, 128), BF16),
             V((8, CLS, 32, 128), BF16), V((8, 32, CLS * NXH), BF16), V((8, 32, CLS * NXH), BF16),
             V((K, 64), F32), V((CLS, 32, 512), BF16),
             dma((10,)), dma((3,)), dma((3,)), dma, dma, dma, dma,
             dma, dma((3, 3)), dma, dma((3,)), dma, dma, dma, dma((3, 3)), dma, dma((3,)),
-            dma((2,)), dma((2,)),
+            dma((2,)), dma((2,)), dma, dma,
         ],
         compiler_params=pltpu.CompilerParams(
             collective_id=0, has_side_effects=True, vmem_limit_bytes=60 * 2**20

time: 53.4 us -> 50.2 us (0.940)
  Pallas kernels: 52.6 us -> 49.5 us
    pallas_call x1, Pallas kernels: 50.9 us -> 47.7 us  [body(): pl.pallas_call(kernel, out_shape=(jax.ShapeDtypeStruct((K, 64), F32), jax...]
where the time goes in v1:
time: 50.2 us; the launch traced here: 50.1 us
  Pallas kernels  49.5 us (99%)
  between operations  0.64 us (1%)
    pallas_call x1, Pallas kernels, body(): pl.pallas_call(kernel, out_shape=(jax.ShapeDtypeStruct((K, 64), F32), jax...  47.7 us
    pallas_call x1, Pallas kernels, body(): pl.pallas_call(place, out_shape=tuple((jax.ShapeDtypeStruct(a.shape, a.dt...  1.75 us

profile of v1, /device:TPU:1, one launch (start us, length us, event | category | flops | bytes accessed | tf_op | source)
XLA Modules:
  0.0 50.1 jit_solution(15916478061698356266)
XLA Ops:
  0.6 47.7 %shard_map.94 = (f32[4,64]{1,0:T(4,128)}, bf16[4,32,1024]{2,1,0:T(8,128)(2,1)}, bf16[4,32,512]{2,1,0:T(8,128)(2,1)}) custom-call(bf16[4,32,1024]{2,1,0:T(8,128)(2,1)} %volume.1, bf16[64,16384]{1,0:T(8,128)(2,1)} %images.1, f32[1,64]{1,0:T(1,128)} %bitcast.8, f32[128,128]{1,0:T(8,128)} %bitcast.5, s32[4,64]{1,0:T(4,128)} %bitcast.6, s32[4,64]{1,0:T(4,128)} %bitcast.7, ...), custom_call_target="tpu_custom_call" | custom-call | tf_op jit(solution)/shard_map/pallas_call | solution.py:460
  48.4 1.7 %shard_map.95 = (f32[4,64]{1,0:T(4,128)}, bf16[4,32,1024]{2,1,0:T(8,128)(2,1)}, bf16[4,32,512]{2,1,0:T(8,128)(2,1)}) custom-call(f32[4,64]{1,0:T(4,128)} %get-tuple-element.9.weights, bf16[4,32,1024]{2,1,0:T(8,128)(2,1)} %get-tuple-element.10.data, bf16[4,32,512]{2,1,0:T(8,128)(2,1)} %get-tuple-element.11.squares), custom_call_target="tpu_custom_call" | custom-call | tf_op jit(solution)/shard_map/pallas_call | solution.py:495

commit v2 on v1

--- a/solution.py
+++ b/solution.py
@@ -33,6 +33,7 @@
 PLACE_OF = {step: i for i, step in enumerate(PLACES)}
 BACK_OF = [PLACE_OF[(-a) % 4, (-b) % 4] for a, b in PLACES]
 CLASSES = ((0, 5), (5, 11), (11, 16))
+RS_CLASSES = ((0, 11), (11, 16))
 CLASS_OF = [0] * 5 + [1] * 6 + [2] * 5
 
 
@@ -319,8 +320,8 @@
             parts[0, dx, PLACE_OF[dy, dz]] = piece[0:THIRD]
             parts[1, dy, PLACE_OF[dx, dz]] = piece[THIRD : 2 * THIRD]
             parts[2, dz, PLACE_OF[dx, dy]] = piece[2 * THIRD :]
-    for i in (2, 1, 0):
-        low, high = CLASSES[i]
+    for i in (1, 0):
+        low, high = RS_CLASSES[i]
         for d in (2, 1, 3):
             for t in range(3):
                 send(
@@ -329,7 +330,7 @@
                 )
     rings = [
         [due(incoming.at[t, :, low:high], rs_recv.at[t, i]) for t in range(3)]
-        for i, (low, high) in enumerate(CLASSES)
+        for i, (low, high) in enumerate(RS_CLASSES)
     ]
     due(incoming, rs_send)
 
@@ -365,8 +366,8 @@
     due(sq_part.at[0:7], sq_send)
     vol_parts = due(sq_in.at[0:7], sq_recv)
 
-    for i in (2, 1, 0):
-        low, high = CLASSES[i]
+    for i in (1, 0):
+        low, high = RS_CLASSES[i]
         for t in range(3):
             rings[i][t]()
             for place in range(high - 1, low - 1, -1):

time: 50.2 us -> 49.8 us (level)
  no operation moved by 1% of the time
where the time goes in v2:
time: 49.8 us; the launch traced here: 49.7 us
  Pallas kernels  49.1 us (99%)
  between operations  0.64 us (1%)
    pallas_call x1, Pallas kernels, body(): pl.pallas_call(kernel, out_shape=(jax.ShapeDtypeStruct((K, 64), F32), jax...  47.3 us
    pallas_call x1, Pallas kernels, body(): pl.pallas_call(place, out_shape=tuple((jax.ShapeDtypeStruct(a.shape, a.dt...  1.75 us

profile of v2, /device:TPU:1, one launch (start us, length us, event | category | flops | bytes accessed | tf_op | source)
XLA Modules:
  0.0 49.7 jit_solution(15302589800725219896)
XLA Ops:
  0.6 47.3 %shard_map.94 = (f32[4,64]{1,0:T(4,128)}, bf16[4,32,1024]{2,1,0:T(8,128)(2,1)}, bf16[4,32,512]{2,1,0:T(8,128)(2,1)}) custom-call(bf16[4,32,1024]{2,1,0:T(8,128)(2,1)} %volume.1, bf16[64,16384]{1,0:T(8,128)(2,1)} %images.1, f32[1,64]{1,0:T(1,128)} %bitcast.8, f32[128,128]{1,0:T(8,128)} %bitcast.5, s32[4,64]{1,0:T(4,128)} %bitcast.6, s32[4,64]{1,0:T(4,128)} %bitcast.7, ...), custom_call_target="tpu_custom_call" | custom-call | tf_op jit(solution)/shard_map/pallas_call | solution.py:461
  48.0 1.7 %shard_map.95 = (f32[4,64]{1,0:T(4,128)}, bf16[4,32,1024]{2,1,0:T(8,128)(2,1)}, bf16[4,32,512]{2,1,0:T(8,128)(2,1)}) custom-call(f32[4,64]{1,0:T(4,128)} %get-tuple-element.9.weights, bf16[4,32,1024]{2,1,0:T(8,128)(2,1)} %get-tuple-element.10.data, bf16[4,32,512]{2,1,0:T(8,128)(2,1)} %get-tuple-element.11.squares), custom_call_target="tpu_custom_call" | custom-call | tf_op jit(solution)/shard_map/pallas_call | solution.py:496

commit v3 on v2

--- a/solution.py
+++ b/solution.py
@@ -215,7 +215,7 @@
 
     local_images()
     sibling_images()
-    lax.fori_loop(0, 8, prepare, 0)
+    lax.fori_loop(0, 4, prepare, 0)
 
     lane24 = lax.broadcasted_iota(jnp.int32, (POSES, 128), 1)
     offset = jnp.sum(jnp.where(lane24 == row, slab_in[...].astype(F32), 0.0), axis=1, keepdims=True)
@@ -249,7 +249,7 @@
         for i, (low, high) in enumerate(CLASSES)
     ]
     due(sl.at[:, 0, 0:15], ag_send)
-    lax.fori_loop(8, 24, prepare, 0)
+    lax.fori_loop(4, 20, prepare, 0)
 
     for i, (low, high) in enumerate(CLASSES):
         for t in range(3):
@@ -261,7 +261,7 @@
                 )
     rest = [due(sl.at[t, 1:4], ring_recv.at[t]) for t in range(3)]
     due(sl.at[:, 1:4], ring_send)
-    lax.fori_loop(24, 64, prepare, 0)
+    lax.fori_loop(20, 64, prepare, 0)
 
     for arrived in rest:
         arrived()

time: 49.8 us -> 49.7 us (level)
  no operation moved by 1% of the time
where the time goes in v3:
time: 49.7 us; the launch traced here: 49.6 us
  Pallas kernels  48.9 us (98%)
  between operations  0.64 us (1%)
    pallas_call x1, Pallas kernels, body(): pl.pallas_call(kernel, out_shape=(jax.ShapeDtypeStruct((K, 64), F32), jax...  47.2 us
    pallas_call x1, Pallas kernels, body(): pl.pallas_call(place, out_shape=tuple((jax.ShapeDtypeStruct(a.shape, a.dt...  1.75 us

profile of v3, /device:TPU:1, one launch (start us, length us, event | category | flops | bytes accessed | tf_op | source)
XLA Modules:
  0.0 49.6 jit_solution(14617289378490693881)
XLA Ops:
  0.6 47.2 %shard_map.94 = (f32[4,64]{1,0:T(4,128)}, bf16[4,32,1024]{2,1,0:T(8,128)(2,1)}, bf16[4,32,512]{2,1,0:T(8,128)(2,1)}) custom-call(bf16[4,32,1024]{2,1,0:T(8,128)(2,1)} %volume.1, bf16[64,16384]{1,0:T(8,128)(2,1)} %images.1, f32[1,64]{1,0:T(1,128)} %bitcast.8, f32[128,128]{1,0:T(8,128)} %bitcast.5, s32[4,64]{1,0:T(4,128)} %bitcast.6, s32[4,64]{1,0:T(4,128)} %bitcast.7, ...), custom_call_target="tpu_custom_call" | custom-call | tf_op jit(solution)/shard_map/pallas_call | solution.py:461
  47.8 1.7 %shard_map.95 = (f32[4,64]{1,0:T(4,128)}, bf16[4,32,1024]{2,1,0:T(8,128)(2,1)}, bf16[4,32,512]{2,1,0:T(8,128)(2,1)}) custom-call(f32[4,64]{1,0:T(4,128)} %get-tuple-element.9.weights, bf16[4,32,1024]{2,1,0:T(8,128)(2,1)} %get-tuple-element.10.data, bf16[4,32,512]{2,1,0:T(8,128)(2,1)} %get-tuple-element.11.squares), custom_call_target="tpu_custom_call" | custom-call | tf_op jit(solution)/shard_map/pallas_call | solution.py:496
